TPU v7x, 128 devices: a whole 4x4x4 slice. The times are simulated.
128 devices in a mesh: seq: 32 (over y, z, core), head: 4 (over x).
Axes of the slice: x: 4, y: 4, z: 4, core: 2. Of those that a mesh axis runs over, the one named last changes fastest.
Arguments:
- query_rows: bfloat16 [32768, 5120], P(('seq', 'head')), may hold values from -6 to 6
- key_rows: bfloat16 [32768, 5120], P(('seq', 'head')), may hold values from -6 to 6
- value_rows: bfloat16 [32768, 5120], P(('seq', 'head')), may hold values from -6 to 6
- log_decay: bfloat16 [32768, 40], P(('seq', 'head')), may hold values from -1 to 0
- documents: int32 [32768], replicated, may hold values from 0 to 2, as said below
- norm_gain: float32 [5120], replicated, may hold values from 0.25 to 1.75
Outputs:
- attended: bfloat16 [32768, 5120], P(('seq', 'head'))
Inputs may be any that keep to these rules, and one draw needn't show every extreme that they name: `documents`: document numbers never fall along the tokens and each of the 3 numbers occurs.
All inputs are finite; a program needn't handle non-finite values.
Results may differ from a plain program's by a relative error of at most 0.0056.
Values may be sent and summed in bfloat16 or wider, within the bound.
No kernel may reach another device: no remote copies, remote signals or barrier semaphores. Data moves between devices by JAX's collectives and lax.ppermute only.
A program may use at most 640 MiB of HBM per device.

v0:
```python
import jax
import jax.numpy as jnp
from jax import lax
from jax.sharding import PartitionSpec as P

BLOCK = 256


def prefix(part, axis, combine, identity):
    place = lax.axis_index(axis)
    gathered = jax.tree.map(lambda a: lax.all_gather(a, axis), part)
    state = jax.tree.map(lambda a, e: jnp.zeros_like(a) + jnp.asarray(e, a.dtype), part, identity)

    def one(lap, state):
        return combine(
            state, jax.tree.map(lambda a: lax.dynamic_index_in_dim(a, lap, 0, False), gathered)
        )

    return lax.fori_loop(0, place, one, state)


def combine_states(earlier, later):
    return (earlier[0] * later[0], later[0][:, None, None] * earlier[1] + later[1])


def block_local(query_blocks, key_blocks, value_blocks, cumulative, doc_blocks):
    span = query_blocks.shape[1]
    scores = jnp.einsum(
        "nchd,nshd->nhcs", query_blocks, key_blocks, preferred_element_type=jnp.float32
    )
    cum_heads = jnp.swapaxes(cumulative, 1, 2)
    exponent = cum_heads[:, :, :, None] - cum_heads[:, :, None, :]
    causal = jnp.arange(span)[:, None] >= jnp.arange(span)[None, :]
    allowed = (causal[None] & (doc_blocks[:, :, None] == doc_blocks[:, None, :]))[:, None]
    decay_mask = jnp.where(allowed, jnp.exp(jnp.where(allowed, exponent, 0.0)), 0.0)
    weights = (scores * decay_mask).astype(jnp.bfloat16)
    return jnp.einsum("nhcs,nshd->nchd", weights, value_blocks, preferred_element_type=jnp.float32)


def attend(query, keyed, valued, decays, documents, first_row, gain_group, prefix_fn):
    row_count = query.shape[0]
    head_count = decays.shape[1]
    head_width = query.shape[1] // head_count
    block_count = row_count // BLOCK
    query_blocks = query.reshape(block_count, BLOCK, head_count, head_width)
    key_blocks = keyed.reshape(block_count, BLOCK, head_count, head_width)
    value_blocks = valued.reshape(block_count, BLOCK, head_count, head_width)
    cumulative = jnp.cumsum(
        decays.astype(jnp.float32).reshape(block_count, BLOCK, head_count), axis=1
    )
    local_docs = lax.dynamic_slice_in_dim(documents, first_row, row_count)
    doc_before = lax.dynamic_slice_in_dim(documents, jnp.maximum(first_row - 1, 0), 1)
    doc_blocks = local_docs.reshape(block_count, BLOCK)
    previous = jnp.concatenate([doc_before, doc_blocks[:-1, -1]])
    usable = (doc_blocks == previous[:, None]).astype(jnp.float32)
    final_cum = cumulative[:, -1, :]
    factor = jnp.exp(final_cum) * (doc_blocks[:, -1] == previous).astype(jnp.float32)[:, None]
    same_last = (doc_blocks == doc_blocks[:, -1:]).astype(jnp.float32)
    key_scale = jnp.exp(final_cum[:, None, :] - cumulative) * same_last[:, :, None]
    key_decayed = (key_blocks.astype(jnp.float32) * key_scale[..., None]).astype(jnp.bfloat16)
    block_state = jnp.einsum(
        "nchd,nche->nhde", key_decayed, value_blocks, preferred_element_type=jnp.float32
    )
    query_decayed = (
        query_blocks.astype(jnp.float32) * (jnp.exp(cumulative) * usable[:, :, None])[..., None]
    ).astype(jnp.bfloat16)

    def local_advance(carry, item):
        decay_so_far, state_so_far = carry
        block_factor, block_update = item
        return (
            (
                decay_so_far * block_factor,
                block_factor[:, None, None] * state_so_far + block_update,
            ),
            (decay_so_far, state_so_far),
        )

    start_carry = (
        jnp.ones((head_count,), jnp.float32),
        jnp.zeros((head_count, head_width, head_width), jnp.float32),
    )
    summary, entering = lax.scan(local_advance, start_carry, (factor, block_state))
    incoming = prefix_fn(summary)[1]

    def advance(carried_state, item):
        query_one, key_one, value_one, cum_one, doc_one, decayed_one, factor_one, update_one = item
        within = block_local(
            query_one[None], key_one[None], value_one[None], cum_one[None], doc_one[None]
        )[0]
        carried = jnp.einsum(
            "chd,hde->che",
            decayed_one,
            carried_state.astype(jnp.bfloat16),
            preferred_element_type=jnp.float32,
        )
        return (factor_one[:, None, None] * carried_state + update_one, within + carried)

    _, outputs = lax.scan(
        advance,
        incoming,
        (
            query_blocks,
            key_blocks,
            value_blocks,
            cumulative,
            doc_blocks,
            query_decayed,
            factor,
            block_state,
        ),
    )
    mean_square = jnp.mean(outputs * outputs, axis=-1, keepdims=True)
    normed = outputs * lax.rsqrt(mean_square + 1e-05) * gain_group.reshape(head_count, head_width)
    return normed.astype(jnp.bfloat16).reshape(row_count, head_count * head_width)


def body(query_rows, key_rows, value_rows, log_decay, documents, norm_gain):
    query, keyed, valued, decays = (
        lax.all_to_all(query_rows, "head", split_axis=1, concat_axis=0, tiled=True),
        lax.all_to_all(key_rows, "head", split_axis=1, concat_axis=0, tiled=True),
        lax.all_to_all(value_rows, "head", split_axis=1, concat_axis=0, tiled=True),
        lax.all_to_all(log_decay, "head", split_axis=1, concat_axis=0, tiled=True),
    )
    row_count = query.shape[0]
    group_width = query.shape[1]
    first_row = lax.axis_index("seq") * row_count
    gain_group = lax.dynamic_slice_in_dim(
        norm_gain, lax.axis_index("head") * group_width, group_width
    )

    def prefix_group(summary):
        identity = (jnp.ones_like(summary[0]), jnp.zeros_like(summary[1]))
        return prefix((summary[0], summary[1]), "seq", combine_states, identity)

    grouped = attend(query, keyed, valued, decays, documents, first_row, gain_group, prefix_group)
    return lax.all_to_all(grouped, "head", split_axis=0, concat_axis=1, tiled=True)


def solution(mesh):
    placed = (
        P(("seq", "head"), None),
        P(("seq", "head"), None),
        P(("seq", "head"), None),
        P(("seq", "head"), None),
        P(),
        P(),
    )
    return jax.shard_map(
        body, mesh=mesh, in_specs=placed, out_specs=P(("seq", "head"), None), check_vma=False
    )
```

profile of v0, /device:TPU:121, one launch (start us, length us, event | category | flops | bytes accessed | tf_op | source)
XLA Modules:
  0.0 299.5 jit_solution(4036128251627386428)
XLA Ops:
  7.9 4.0 %all-to-all-start = ((bf16[256,4,10]{0,2,1:T(8,128)(2,1)}), bf16[256,4,10]{0,2,1:T(8,128)(2,1)S(1)}, u32[]{:S(2)}, u32[]{:S(2)}) async-start(bf16[256,4,10]{0,2,1:T(8,128)(2,1)} %all_to_all.60), calls=%async_computation | async-start | bytes 65536 | tf_op jit(solution)/shard_map/all_to_all | solution.py:123
  11.9 4.4 %copy.88 = bf16[256,5120]{0,1:T(8,128)(2,1)} copy(bf16[256,5120]{1,0:T(8,128)(2,1)} %param.13) | data formatting | bytes 5242880 | tf_op args[1]
  16.3 4.2 %all-to-all-start.1 = ((bf16[256,4,1280]{0,2,1:T(8,128)(2,1)}), bf16[256,4,1280]{0,2,1:T(8,128)(2,1)S(1)}, u32[]{:S(2)}, u32[]{:S(2)}) async-start(bf16[256,4,1280]{0,2,1:T(8,128)(2,1)} %bitcast.125), calls=%async_computation.1 | async-start | bytes 5242880 | tf_op jit(solution)/shard_map/all_to_all | solution.py:121
  20.5 4.4 %copy.91 = bf16[256,5120]{0,1:T(8,128)(2,1)} copy(bf16[256,5120]{1,0:T(8,128)(2,1)} %param.14) | data formatting | bytes 5242880 | tf_op args[2]
  24.9 26.1 %all-to-all-done.1 = bf16[256,4,1280]{0,2,1:T(8,128)(2,1)S(1)} async-done(((bf16[256,4,1280]{0,2,1:T(8,128)(2,1)}), bf16[256,4,1280]{0,2,1:T(8,128)(2,1)S(1)}, u32[]{:S(2)}, u32[]{:S(2)}) %all-to-all-start.1) | async-done | bytes 2621472 | tf_op jit(solution)/shard_map/all_to_all | solution.py:121
  52.5 4.6 %all-to-all-start.2 = ((bf16[256,4,1280]{0,2,1:T(8,128)(2,1)}), bf16[256,4,1280]{0,2,1:T(8,128)(2,1)}, u32[]{:S(2)}, u32[]{:S(2)}) async-start(bf16[256,4,1280]{0,2,1:T(8,128)(2,1)} %bitcast.123), calls=%async_computation.2 | async-start | bytes 5242880 | tf_op jit(solution)/shard_map/all_to_all | solution.py:122
  61.4 2.3 reduce-window.6
  64.5 22.2 %all-to-all-done.2 = bf16[256,4,1280]{0,2,1:T(8,128)(2,1)} async-done(((bf16[256,4,1280]{0,2,1:T(8,128)(2,1)}), bf16[256,4,1280]{0,2,1:T(8,128)(2,1)}, u32[]{:S(2)}, u32[]{:S(2)}) %all-to-all-start.2) | async-done | bytes 2621472 | tf_op jit(solution)/shard_map/all_to_all | solution.py:122
  86.7 3.4 %fusion.27 = f32[4,10,128,128]{3,2,1,0:T(8,128)S(1)} fusion(bf16[4,256,10,128]{1,3,2,0:T(8,128)(2,1)} %bitcast.27, bf16[4,256,10,128]{1,3,2,0:T(8,128)(2,1)} %bitcast.119, f32[4,256,10]{1,2,0:T(8,128)S(1)} %copy.90), kind=kOutput, calls=%fused_computation.41 | convolution fusion | flops 339476480 | bytes 7905280 | tf_op jit(solution)/shard_map/nchd,nche->nhde/dot_general | solution.py:61
  91.7 4.6 %copy.93 = bf16[256,5120]{0,1:T(8,128)(2,1)} copy(bf16[256,5120]{1,0:T(8,128)(2,1)} %param.12) | data formatting | bytes 5242880 | tf_op args[0]
  96.3 3.8 %all-to-all-start.3 = ((bf16[256,4,1280]{0,2,1:T(8,128)(2,1)}), bf16[256,4,1280]{0,2,1:T(8,128)(2,1)S(1)}, u32[]{:S(2)}, u32[]{:S(2)}) async-start(bf16[256,4,1280]{0,2,1:T(8,128)(2,1)} %bitcast.124), calls=%async_computation.3 | async-start | bytes 5242880 | tf_op jit(solution)/shard_map/all_to_all | solution.py:120
  101.9 63.2 %all-reduce = f32[320]{0:T(512)S(1)} all-reduce(f32[320]{0:T(512)S(1)} %dynamic-update-slice), channel_id=2, replica_groups=mesh['seq'=32,'head'=4] {'seq'}, use_global_device_ids=true, to_apply=%add | all-reduce | flops 320 | bytes 2560
  167.5 7.4 %all-gather.4.cloned.1.call-done = f32[320,128,128]{2,1,0:T(8,128)} async-done(((f32[10,128,128]{2,1,0:T(8,128)}), f32[320,128,128]{2,1,0:T(8,128)}) %all-gather.4.cloned.1.call-update) | async-done | bytes 20971536 | tf_op jit(solution)/shard_map/all_gather | solution.py:11
  174.9 40.4 %while.37 = (s32[]{:T(128)}, f32[10,128,128]{2,1,0:T(8,128)S(1)}, s32[]{:T(128)}, f32[32,10]{1,0:T(8,128)S(1)}, f32[32,10,128,128]{3,2,1,0:T(8,128)}, /*index=5*/s32[]{:T(128)}, s32[]{:T(128)}, s32[]{:T(128)}) while((s32[]{:T(128)}, f32[10,128,128]{2,1,0:T(8,128)S(1)}, s32[]{:T(128)}, f32[32,10]{1,0:T(8,128)S(1)}, ...), condition=%wide.region_5.6_spmd, body=%wide.region_4.5_spmd.sunk | while | flops 327685 | bytes 1966327 | solution.py:19
  215.4 27.1 %while.38 = (s32[]{:T(128)}, f32[10,128,128]{2,1,0:T(8,128)S(1)}, f32[4,256,10,128]{1,3,2,0:T(8,128)}, f32[4,10]{1,0:T(4,128)S(1)}, f32[4,10,128,128]{3,2,1,0:T(...) while((s32[]{:T(128)}, f32[10,128,128]{2,1,0:T(8,128)S(1)}, ...), condition=%wide.region_7.8_spmd, body=%wide.region_6.7_spmd.sunk | while | flops 423723008 | bytes 9385725 | solution.py:99
  217.0 3.8 %fusion.48 = f32[4,256,10,128]{1,3,2,0:T(8,128)} fusion(f32[4,256,10,128]{1,3,2,0:T(8,128)} %get-tuple-element.454, s32[]{:T(128)} %get-tuple-element.452, f32[256,10,128]{0,2,1:T(8,128)S(1)} %convolution_bitcast_fusion.3, f32[10,256]{1,0:T(8,128)S(1)} %bitcast.130, pred[256,256]{1,0:T(8,128)(4,1)S(1)} %fusion.47, ...), kind=kOutput, calls=%fused_computation.6.clone.1 | convolution fusion | flops 339148800 | bytes 4687872 | tf_op jit(solution)/shard_map/while/body/eval_jaxpr/nhcs,nshd->nchd/dot_general | solution.py:37
  223.8 3.9 %fusion.48 = f32[4,256,10,128]{1,3,2,0:T(8,128)} fusion(f32[4,256,10,128]{1,3,2,0:T(8,128)} %get-tuple-element.454, s32[]{:T(128)} %get-tuple-element.452, f32[256,10,128]{0,2,1:T(8,128)S(1)} %convolution_bitcast_fusion.3, f32[10,256]{1,0:T(8,128)S(1)} %bitcast.130, pred[256,256]{1,0:T(8,128)(4,1)S(1)} %fusion.47, ...), kind=kOutput, calls=%fused_computation.6.clone.1 | convolution fusion | flops 339148800 | bytes 4687872 | tf_op jit(solution)/shard_map/while/body/eval_jaxpr/nhcs,nshd->nchd/dot_general | solution.py:37
  230.6 3.8 %fusion.48 = f32[4,256,10,128]{1,3,2,0:T(8,128)} fusion(f32[4,256,10,128]{1,3,2,0:T(8,128)} %get-tuple-element.454, s32[]{:T(128)} %get-tuple-element.452, f32[256,10,128]{0,2,1:T(8,128)S(1)} %convolution_bitcast_fusion.3, f32[10,256]{1,0:T(8,128)S(1)} %bitcast.130, pred[256,256]{1,0:T(8,128)(4,1)S(1)} %fusion.47, ...), kind=kOutput, calls=%fused_computation.6.clone.1 | convolution fusion | flops 339148800 | bytes 4687872 | tf_op jit(solution)/shard_map/while/body/eval_jaxpr/nhcs,nshd->nchd/dot_general | solution.py:37
  237.3 3.9 %fusion.48 = f32[4,256,10,128]{1,3,2,0:T(8,128)} fusion(f32[4,256,10,128]{1,3,2,0:T(8,128)} %get-tuple-element.454, s32[]{:T(128)} %get-tuple-element.452, f32[256,10,128]{0,2,1:T(8,128)S(1)} %convolution_bitcast_fusion.3, f32[10,256]{1,0:T(8,128)S(1)} %bitcast.130, pred[256,256]{1,0:T(8,128)(4,1)S(1)} %fusion.47, ...), kind=kOutput, calls=%fused_computation.6.clone.1 | convolution fusion | flops 339148800 | bytes 4687872 | tf_op jit(solution)/shard_map/while/body/eval_jaxpr/nhcs,nshd->nchd/dot_general | solution.py:37
  242.5 3.2 %multiply_reduce_fusion = f32[4,256,10]{1,2,0:T(8,128)S(1)} fusion(f32[4,256,10,128]{1,3,2,0:T(8,128)} %get-tuple-element.137), kind=kLoop, calls=%fused_computation.38 | loop fusion | flops 2611200 | bytes 5283840 | tf_op jit(solution)/shard_map/reduce_sum | solution.py:113
  247.2 2.6 copy.99
  249.8 35.9 %all_to_all.80 = bf16[4,256,1280]{2,1,0:T(8,128)(2,1)S(1)} all-to-all(bf16[4,256,1280]{2,1,0:T(8,128)(2,1)} %copy.99), channel_id=1, replica_groups=mesh['seq'=32,'head'=4] {'head'}, dimensions={0} | all-to-all | bytes 5242880 | tf_op jit(solution)/shard_map/all_to_all | solution.py:137
  285.7 2.5 copy.100
  288.2 4.4 %copy.101 = bf16[256,5120]{1,0:T(8,128)(2,1)} copy(bf16[256,5120]{0,1:T(8,128)(2,1)} %bitcast.126) | data formatting | bytes 5242880 | tf_op jit(solution)/shard_map/all_to_all | solution.py:137
  (158 shorter events, 65.8 us)
Async XLA Ops:
  6.5 95.0 %copy-start = (f32[5120]{0:T(1024)S(1)}, f32[5120]{0:T(1024)}, u32[]{:S(2)}) copy-start(f32[5120]{0:T(1024)} %param.17) | copy-start | bytes 61444
  7.9 8.4 %all-to-all-start = ((bf16[256,4,10]{0,2,1:T(8,128)(2,1)}), bf16[256,4,10]{0,2,1:T(8,128)(2,1)S(1)}, u32[]{:S(2)}, u32[]{:S(2)}) async-start(bf16[256,4,10]{0,2,1:T(8,128)(2,1)} %all_to_all.60), calls=%async_computation | async-start | bytes 65536 | tf_op jit(solution)/shard_map/all_to_all | solution.py:123
  16.3 34.7 %all-to-all-start.1 = ((bf16[256,4,1280]{0,2,1:T(8,128)(2,1)}), bf16[256,4,1280]{0,2,1:T(8,128)(2,1)S(1)}, u32[]{:S(2)}, u32[]{:S(2)}) async-start(bf16[256,4,1280]{0,2,1:T(8,128)(2,1)} %bitcast.125), calls=%async_computation.1 | async-start | bytes 5242880 | tf_op jit(solution)/shard_map/all_to_all | solution.py:121
  51.0 1.5 copy-start.5
  52.5 34.2 %all-to-all-start.2 = ((bf16[256,4,1280]{0,2,1:T(8,128)(2,1)}), bf16[256,4,1280]{0,2,1:T(8,128)(2,1)}, u32[]{:S(2)}, u32[]{:S(2)}) async-start(bf16[256,4,1280]{0,2,1:T(8,128)(2,1)} %bitcast.123), calls=%async_computation.2 | async-start | bytes 5242880 | tf_op jit(solution)/shard_map/all_to_all | solution.py:122
  57.1 117.8 %all-gather.4.cloned.1.call-start = ((), (), s32[]{:S(2)}) async-start(), calls=%async_computation.5 | async-start | bytes 21626880 | tf_op jit(solution)/shard_map/all_gather | solution.py:11
  90.8 0.9 copy-start.3
  90.8 5.5 %copy-start.2 = (f32[4,10,128,128]{3,2,1,0:T(8,128)}, f32[4,10,128,128]{3,2,1,0:T(8,128)S(1)}, u32[]{:S(2)}) copy-start(f32[4,10,128,128]{3,2,1,0:T(8,128)S(1)} %get-tuple-element.477) | copy-start | bytes 7864324
  96.3 3.8 %copy-start.7 = (u32[128]{0:T(128)S(1)}, u32[128]{0:T(128)}, u32[]{:S(2)}) copy-start(u32[128]{0:T(128)} %constant.83) | copy-start | bytes 1540
  96.3 68.9 %all-to-all-start.3 = ((bf16[256,4,1280]{0,2,1:T(8,128)(2,1)}), bf16[256,4,1280]{0,2,1:T(8,128)(2,1)S(1)}, u32[]{:S(2)}, u32[]{:S(2)}) async-start(bf16[256,4,1280]{0,2,1:T(8,128)(2,1)} %bitcast.124), calls=%async_computation.3 | async-start | bytes 5242880 | tf_op jit(solution)/shard_map/all_to_all | solution.py:120
  165.2 2.3 copy-start.6
  242.5 4.0 %copy-start.4 = (f32[4,256,10,128]{1,3,2,0:T(8,128)S(1)}, f32[4,256,10,128]{1,3,2,0:T(8,128)}, u32[]{:S(2)}) copy-start(f32[4,256,10,128]{1,3,2,0:T(8,128)} %get-tuple-element.137) | copy-start | bytes 15728644
  288.2 4.4 %copy-start.1 = (f32[5120]{0:T(1024)S(1)}, f32[5120]{0:T(1024)}, u32[]{:S(2)}) copy-start(f32[5120]{0:T(1024)} %param.17) | copy-start | bytes 61444
Sparse Core Ops, SparseCore 0:
  91.8 82.9 all-gather.3
where the time goes:
time: 302 us; the launch traced here: 299 us
  blocking collectives  99.1 us (33%)
  waiting for transfers between devices  55.6 us (18%)
  other arithmetic  55.5 us (18%)
  local copies, waits for them, and re-layouts  32 us (11%)
  matrix products  24.7 us (8%)
  starting transfers between devices  16.6 us (5%)
  between operations  14.4 us (5%)
    unnamed x1, blocking collectives  63.2 us
    add x31, other arithmetic, combine_states(): later[0][:, None, None] * earlier[1] + later[1]  38.9 us
    all_to_all x1, blocking collectives, body(): lax.all_to_all(grouped, 'head', split_axis=0, concat_axis=1, tiled=True)  35.9 us
    all_to_all x1, waiting for transfers between devices, body(): lax.all_to_all(key_rows, 'head', split_axis=1, concat_axis=0, tiled=True)  26.1 us
    all_to_all x1, waiting for transfers between devices, body(): lax.all_to_all(value_rows, 'head', split_axis=1, concat_axis=0, tiled=True)  22.2 us
    unnamed x22, local copies, waits for them, and re-layouts  17.4 us
    dot_general x4, matrix products, block_local(): jnp.einsum('nhcs,nshd->nchd', weights, value_blocks, preferred_element_ty...  15.5 us
    all_to_all x3, local copies, waits for them, and re-layouts, body(): lax.all_to_all(grouped, 'head', split_axis=0, concat_axis=1, tiled=True)  9.5 us
  transfers between devices with their start and end apart: 5, of which 3 were waited for; matrix products, arithmetic and copies ran while one was open for 8% of the time, Pallas kernels for 0%

commit v1 on v0

--- a/solution.py
+++ b/solution.py
@@ -4,6 +4,29 @@
 from jax.sharding import PartitionSpec as P
 
 BLOCK = 256
+
+
+def in_blocks(value, dim, count):
+    shape = value.shape
+    blocks = value.reshape(*shape[:dim], count, shape[dim] // count, *shape[dim + 1 :])
+    return jnp.moveaxis(blocks, dim, 0)
+
+
+def laid_out(pieces, dim):
+    lengths = list(pieces.shape[1:])
+    lengths[dim] *= pieces.shape[0]
+    return jnp.moveaxis(pieces, 0, dim).reshape(lengths)
+
+
+def pairwise_exchange(x, axis, split_dim, concat_dim):
+    count, position = (lax.axis_size(axis), lax.axis_index(axis))
+    parts = in_blocks(x, split_dim, count)
+    outs = [parts[position]]
+    for step in range(1, count):
+        sent = parts[position ^ step]
+        outs.append(lax.ppermute(sent, axis, [(i, i ^ step) for i in range(count)]))
+    parts = jnp.stack(outs)[position ^ jnp.arange(count)]
+    return laid_out(parts, concat_dim)
 
 
 def prefix(part, axis, combine, identity):
@@ -118,7 +141,7 @@
 def body(query_rows, key_rows, value_rows, log_decay, documents, norm_gain):
     query, keyed, valued, decays = (
         lax.all_to_all(query_rows, "head", split_axis=1, concat_axis=0, tiled=True),
-        lax.all_to_all(key_rows, "head", split_axis=1, concat_axis=0, tiled=True),
+        pairwise_exchange(key_rows, "head", 1, 0),
         lax.all_to_all(value_rows, "head", split_axis=1, concat_axis=0, tiled=True),
         lax.all_to_all(log_decay, "head", split_axis=1, concat_axis=0, tiled=True),
     )

time: 302 us -> 301 us (level)
  waiting for transfers between devices: 55.6 us -> 39.7 us
  local copies, waits for them, and re-layouts: 32 us -> 45.4 us
  other arithmetic: 55.5 us -> 58.9 us
    all_to_all x1 -> x0, waiting for transfers between devices: 26.1 us -> none  [body(): lax.all_to_all(key_rows, 'head', split_axis=1, concat_axis=0, tiled=True)]
    all_to_all x1, waiting for transfers between devices: 0.01 us -> 21.4 us  [body(): lax.all_to_all(log_decay, 'head', split_axis=1, concat_axis=0, tiled=True)]
    all_to_all x1, waiting for transfers between devices: 22.2 us -> 10.9 us  [body(): lax.all_to_all(value_rows, 'head', split_axis=1, concat_axis=0, tiled=True)]
    another operation x7 -> x12, local copies, waits for them, and re-layouts: 0.15 us -> 9.25 us
    gather x0 -> x2, local copies, waits for them, and re-layouts: none -> 8.33 us  [pairwise_exchange(): parts = jnp.stack(outs)[position ^ jnp.arange(count)]]
    all_to_all x1 -> x0, starting transfers between devices: 4.24 us -> none  [body(): lax.all_to_all(key_rows, 'head', split_axis=1, concat_axis=0, tiled=True)]
    ppermute x0 -> x3, starting transfers between devices: none -> 3.86 us  [pairwise_exchange(): outs.append(lax.ppermute(sent, axis, [(i, i ^ step) for i in range(count)]))]
    another operation x4 -> x5, other arithmetic: 2.39 us -> 5.91 us  [the longest x1 3.52 us: pairwise_exchange(): parts = jnp.stack(outs)[position ^ jnp.arange(count)]]
  transfers between devices with their start and end apart: 5 -> 7, of which waited for: 3 -> 3; matrix products, arithmetic and copies ran while one was open for 8% -> 12% of each run, Pallas kernels for 0% -> 0%
where the time goes in v1:
time: 301 us; the launch traced here: 299 us
  blocking collectives  99.1 us (33%)
  other arithmetic  58.9 us (20%)
  local copies, waits for them, and re-layouts  45.4 us (15%)
  waiting for transfers between devices  39.7 us (13%)
  matrix products  24.8 us (8%)
  starting transfers between devices  15.1 us (5%)
  between operations  14.2 us (5%)
    unnamed x1, blocking collectives  63.2 us
    add x31, other arithmetic, combine_states(): later[0][:, None, None] * earlier[1] + later[1]  38.9 us
    all_to_all x1, blocking collectives, body(): lax.all_to_all(grouped, 'head', split_axis=0, concat_axis=1, tiled=True)  35.9 us
    all_to_all x1, waiting for transfers between devices, body(): lax.all_to_all(log_decay, 'head', split_axis=1, concat_axis=0, tiled=True)  21.4 us
    dot_general x4, matrix products, block_local(): jnp.einsum('nhcs,nshd->nchd', weights, value_blocks, preferred_element_ty...  15.5 us
    unnamed x26, local copies, waits for them, and re-layouts  14.1 us
    all_to_all x1, waiting for transfers between devices, body(): lax.all_to_all(value_rows, 'head', split_axis=1, concat_axis=0, tiled=True)  10.9 us
    all_to_all x3, local copies, waits for them, and re-layouts, body(): lax.all_to_all(grouped, 'head', split_axis=0, concat_axis=1, tiled=True)  9.52 us
  transfers between devices with their start and end apart: 7, of which 3 were waited for; matrix products, arithmetic and copies ran while one was open for 12% of the time, Pallas kernels for 0%

profile of v1, /device:TPU:121, one launch (start us, length us, event | category | flops | bytes accessed | tf_op | source)
XLA Modules:
  0.0 298.6 jit_solution(4263559349699299405)
XLA Ops:
  6.5 3.0 copy.121
  21.0 3.7 %all-to-all-start = ((bf16[256,4,10]{0,2,1:T(8,128)(2,1)}), bf16[256,4,10]{0,2,1:T(8,128)(2,1)S(1)}, u32[]{:S(2)}, u32[]{:S(2)}) async-start(bf16[256,4,10]{0,2,1:T(8,128)(2,1)} %all_to_all.48), calls=%async_computation | async-start | bytes 65536 | tf_op jit(solution)/shard_map/all_to_all | solution.py:146
  29.7 21.4 %all-to-all-done = bf16[256,4,10]{0,2,1:T(8,128)(2,1)S(1)} async-done(((bf16[256,4,10]{0,2,1:T(8,128)(2,1)}), bf16[256,4,10]{0,2,1:T(8,128)(2,1)S(1)}, u32[]{:S(2)}, u32[]{:S(2)}) %all-to-all-start) | async-done | bytes 20512 | tf_op jit(solution)/shard_map/all_to_all | solution.py:146
  51.0 3.7 %all-to-all-start.1 = ((bf16[256,4,1280]{0,2,1:T(8,128)(2,1)}), bf16[256,4,1280]{0,2,1:T(8,128)(2,1)S(1)}, u32[]{:S(2)}, u32[]{:S(2)}) async-start(bf16[256,4,1280]{0,2,1:T(8,128)(2,1)} %bitcast.132), calls=%async_computation.1 | async-start | bytes 5242880 | tf_op jit(solution)/shard_map/all_to_all | solution.py:145
  61.8 3.5 %pad_maximum_fusion = bf16[4,256,1280]{2,1,0:T(8,128)(2,1)} fusion(bf16[1,256,1280]{2,1,0:T(8,128)(2,1)} %bitcast.29, bf16[1,256,1280]{2,1,0:T(8,128)(2,1)} %bitcast.27, bf16[1,256,1280]{2,1,0:T(8,128)(2,1)} %bitcast.25, bf16[1,256,1280]{2,1,0:T(8,128)(2,1)} %bitcast.136), kind=kLoop, calls=%fused_computation.43 | loop fusion | flops 3932160 | bytes 5242880 | tf_op jit(solution)/shard_map/stack | solution.py:28
  65.3 4.0 %gather_fusion = bf16[4,256,1280]{2,1,0:T(8,128)(2,1)} fusion(bf16[4,256,1280]{2,1,0:T(8,128)(2,1)} %pad_maximum_fusion, s32[1024]{0:T(1024)S(1)} %pad_clamp_fusion), kind=kCustom, calls=%fused_computation | custom fusion | bytes 5242896 | tf_op jit(solution)/shard_map/gather | solution.py:28
  69.3 4.4 %copy.126 = bf16[4,256,1280]{1,2,0:T(8,128)(2,1)} copy(bf16[4,256,1280]{2,1,0:T(8,128)(2,1)} %gather_fusion) | data formatting | bytes 5242880 | tf_op jit(solution)/shard_map/gather | solution.py:28
  73.6 10.9 %all-to-all-done.1 = bf16[256,4,1280]{0,2,1:T(8,128)(2,1)S(1)} async-done(((bf16[256,4,1280]{0,2,1:T(8,128)(2,1)}), bf16[256,4,1280]{0,2,1:T(8,128)(2,1)S(1)}, u32[]{:S(2)}, u32[]{:S(2)}) %all-to-all-start.1) | async-done | bytes 2621472 | tf_op jit(solution)/shard_map/all_to_all | solution.py:145
  86.1 3.4 %fusion.27 = f32[4,10,128,128]{3,2,1,0:T(8,128)S(1)} fusion(bf16[4,256,10,128]{1,3,2,0:T(8,128)(2,1)} %bitcast.126, bf16[4,256,10,128]{1,3,2,0:T(8,128)(2,1)} %bitcast.128, f32[4,256,10]{1,2,0:T(8,128)S(1)} %copy.128), kind=kOutput, calls=%fused_computation.42 | convolution fusion | flops 339476480 | bytes 7905280 | tf_op jit(solution)/shard_map/nchd,nche->nhde/dot_general | solution.py:84
  91.1 4.6 %copy.131 = bf16[256,5120]{0,1:T(8,128)(2,1)} copy(bf16[256,5120]{1,0:T(8,128)(2,1)} %param.12) | data formatting | bytes 5242880 | tf_op args[0]
  95.7 3.8 %all-to-all-start.2 = ((bf16[256,4,1280]{0,2,1:T(8,128)(2,1)}), bf16[256,4,1280]{0,2,1:T(8,128)(2,1)S(1)}, u32[]{:S(2)}, u32[]{:S(2)}) async-start(bf16[256,4,1280]{0,2,1:T(8,128)(2,1)} %bitcast.133), calls=%async_computation.2 | async-start | bytes 5242880 | tf_op jit(solution)/shard_map/all_to_all | solution.py:143
  101.0 63.2 %all-reduce = f32[320]{0:T(512)S(1)} all-reduce(f32[320]{0:T(512)S(1)} %dynamic-update-slice), channel_id=2, replica_groups=mesh['seq'=32,'head'=4] {'seq'}, use_global_device_ids=true, to_apply=%add | all-reduce | flops 320 | bytes 2560
  166.6 7.4 %all-gather.4.cloned.1.call-done = f32[320,128,128]{2,1,0:T(8,128)} async-done(((f32[10,128,128]{2,1,0:T(8,128)}), f32[320,128,128]{2,1,0:T(8,128)}) %all-gather.4.cloned.1.call-update) | async-done | bytes 20971536 | tf_op jit(solution)/shard_map/all_gather | solution.py:34
  174.1 40.4 %while.37 = (s32[]{:T(128)}, f32[10,128,128]{2,1,0:T(8,128)S(1)}, s32[]{:T(128)}, f32[32,10]{1,0:T(8,128)S(1)}, f32[32,10,128,128]{3,2,1,0:T(8,128)}, /*index=5*/s32[]{:T(128)}, s32[]{:T(128)}, s32[]{:T(128)}) while((s32[]{:T(128)}, f32[10,128,128]{2,1,0:T(8,128)S(1)}, s32[]{:T(128)}, f32[32,10]{1,0:T(8,128)S(1)}, ...), condition=%wide.region_5.6_spmd, body=%wide.region_4.5_spmd.sunk | while | flops 327685 | bytes 1966327 | solution.py:42
  214.5 27.1 %while.38 = (s32[]{:T(128)}, f32[10,128,128]{2,1,0:T(8,128)S(1)}, f32[4,256,10,128]{1,3,2,0:T(8,128)}, f32[4,10]{1,0:T(4,128)S(1)}, f32[4,10,128,128]{3,2,1,0:T(...) while((s32[]{:T(128)}, f32[10,128,128]{2,1,0:T(8,128)S(1)}, ...), condition=%wide.region_7.8_spmd, body=%wide.region_6.7_spmd.sunk | while | flops 423723008 | bytes 9385725 | solution.py:122
  216.2 3.9 %fusion.49 = f32[4,256,10,128]{1,3,2,0:T(8,128)} fusion(f32[4,256,10,128]{1,3,2,0:T(8,128)} %get-tuple-element.469, s32[]{:T(128)} %get-tuple-element.467, f32[256,10,128]{0,2,1:T(8,128)S(1)} %convolution_bitcast_fusion.3, f32[10,256]{1,0:T(8,128)S(1)} %bitcast.143, pred[256,256]{1,0:T(8,128)(4,1)S(1)} %fusion.48, ...), kind=kOutput, calls=%fused_computation.7.clone.1 | convolution fusion | flops 339148800 | bytes 4687872 | tf_op jit(solution)/shard_map/while/body/eval_jaxpr/nhcs,nshd->nchd/dot_general | solution.py:60
  222.9 3.9 %fusion.49 = f32[4,256,10,128]{1,3,2,0:T(8,128)} fusion(f32[4,256,10,128]{1,3,2,0:T(8,128)} %get-tuple-element.469, s32[]{:T(128)} %get-tuple-element.467, f32[256,10,128]{0,2,1:T(8,128)S(1)} %convolution_bitcast_fusion.3, f32[10,256]{1,0:T(8,128)S(1)} %bitcast.143, pred[256,256]{1,0:T(8,128)(4,1)S(1)} %fusion.48, ...), kind=kOutput, calls=%fused_computation.7.clone.1 | convolution fusion | flops 339148800 | bytes 4687872 | tf_op jit(solution)/shard_map/while/body/eval_jaxpr/nhcs,nshd->nchd/dot_general | solution.py:60
  229.7 3.8 %fusion.49 = f32[4,256,10,128]{1,3,2,0:T(8,128)} fusion(f32[4,256,10,128]{1,3,2,0:T(8,128)} %get-tuple-element.469, s32[]{:T(128)} %get-tuple-element.467, f32[256,10,128]{0,2,1:T(8,128)S(1)} %convolution_bitcast_fusion.3, f32[10,256]{1,0:T(8,128)S(1)} %bitcast.143, pred[256,256]{1,0:T(8,128)(4,1)S(1)} %fusion.48, ...), kind=kOutput, calls=%fused_computation.7.clone.1 | convolution fusion | flops 339148800 | bytes 4687872 | tf_op jit(solution)/shard_map/while/body/eval_jaxpr/nhcs,nshd->nchd/dot_general | solution.py:60
  236.5 3.9 %fusion.49 = f32[4,256,10,128]{1,3,2,0:T(8,128)} fusion(f32[4,256,10,128]{1,3,2,0:T(8,128)} %get-tuple-element.469, s32[]{:T(128)} %get-tuple-element.467, f32[256,10,128]{0,2,1:T(8,128)S(1)} %convolution_bitcast_fusion.3, f32[10,256]{1,0:T(8,128)S(1)} %bitcast.143, pred[256,256]{1,0:T(8,128)(4,1)S(1)} %fusion.48, ...), kind=kOutput, calls=%fused_computation.7.clone.1 | convolution fusion | flops 339148800 | bytes 4687872 | tf_op jit(solution)/shard_map/while/body/eval_jaxpr/nhcs,nshd->nchd/dot_general | solution.py:60
  241.7 3.2 %multiply_reduce_fusion = f32[4,256,10]{1,2,0:T(8,128)S(1)} fusion(f32[4,256,10,128]{1,3,2,0:T(8,128)} %get-tuple-element.137), kind=kLoop, calls=%fused_computation.39 | loop fusion | flops 2611200 | bytes 5283840 | tf_op jit(solution)/shard_map/reduce_sum | solution.py:136
  246.4 2.6 copy.137
  249.0 35.9 %all_to_all.64 = bf16[4,256,1280]{2,1,0:T(8,128)(2,1)S(1)} all-to-all(bf16[4,256,1280]{2,1,0:T(8,128)(2,1)} %copy.137), channel_id=1, replica_groups=mesh['seq'=32,'head'=4] {'head'}, dimensions={0} | all-to-all | bytes 5242880 | tf_op jit(solution)/shard_map/all_to_all | solution.py:160
  284.8 2.6 copy.138
  287.4 4.4 %copy.139 = bf16[256,5120]{1,0:T(8,128)(2,1)} copy(bf16[256,5120]{0,1:T(8,128)(2,1)} %bitcast.135) | data formatting | bytes 5242880 | tf_op jit(solution)/shard_map/all_to_all | solution.py:160
  (176 shorter events, 82.6 us)
Async XLA Ops:
  6.5 94.1 %copy-start = (f32[5120]{0:T(1024)S(1)}, f32[5120]{0:T(1024)}, u32[]{:S(2)}) copy-start(f32[5120]{0:T(1024)} %param.17) | copy-start | bytes 61444
  10.9 9.5 %copy-start.8 = (bf16[256,40]{0,1:T(8,128)(2,1)S(1)}, bf16[256,40]{0,1:T(8,128)(2,1)}, u32[]{:S(2)}) copy-start(bf16[256,40]{0,1:T(8,128)(2,1)} %param.15) | copy-start | bytes 61444
  10.9 16.2 %copy-start.7 = (bf16[256,5120]{1,0:T(8,128)(2,1)S(1)}, bf16[256,5120]{1,0:T(8,128)(2,1)}, u32[]{:S(2)}) copy-start(bf16[256,5120]{1,0:T(8,128)(2,1)} %param.14) | copy-start | bytes 7864324
  13.2 48.6 %collective-permute-start = (bf16[256,1280]{1,0:T(8,128)(2,1)}, bf16[256,1280]{1,0:T(8,128)(2,1)}, u32[]{:S(2)}, u32[]{:S(2)}) collective-permute-start(bf16[256,1280]{1,0:T(8,128)(2,1)} %bitcast.137), channel_id=1, source_target_pairs={{0,1},{1,0},{2,3},{3,2},{4,5},{5,4},{6,7},{7,6},{8,9},{9,8},{10,11... | collective-permute-start | bytes 1966088 | tf_op jit(solution)/shard_map/ppermute | solution.py:27
  16.6 45.2 %collective-permute-start.1 = (bf16[256,1280]{1,0:T(8,128)(2,1)}, bf16[256,1280]{1,0:T(8,128)(2,1)}, u32[]{:S(2)}, u32[]{:S(2)}) collective-permute-start(bf16[256,1280]{1,0:T(8,128)(2,1)} %bitcast.138), channel_id=1, source_target_pairs={{0,2},{1,3},{2,0},{3,1},{4,6},{5,7},{6,4},{7,5},{8,10},{9,11},{10,... | collective-permute-start | bytes 1966088 | tf_op jit(solution)/shard_map/ppermute | solution.py:27
  20.1 41.6 %collective-permute-start.2 = (bf16[256,1280]{1,0:T(8,128)(2,1)}, bf16[256,1280]{1,0:T(8,128)(2,1)}, u32[]{:S(2)}, u32[]{:S(2)}) collective-permute-start(bf16[256,1280]{1,0:T(8,128)(2,1)} %bitcast.139), channel_id=1, source_target_pairs={{0,3},{1,2},{2,1},{3,0},{4,7},{5,6},{6,5},{7,4},{8,11},{9,10},{10,... | collective-permute-start | bytes 1966088 | tf_op jit(solution)/shard_map/ppermute | solution.py:27
  21.0 30.1 %all-to-all-start = ((bf16[256,4,10]{0,2,1:T(8,128)(2,1)}), bf16[256,4,10]{0,2,1:T(8,128)(2,1)S(1)}, u32[]{:S(2)}, u32[]{:S(2)}) async-start(bf16[256,4,10]{0,2,1:T(8,128)(2,1)} %all_to_all.48), calls=%async_computation | async-start | bytes 65536 | tf_op jit(solution)/shard_map/all_to_all | solution.py:146
  51.0 33.5 %all-to-all-start.1 = ((bf16[256,4,1280]{0,2,1:T(8,128)(2,1)}), bf16[256,4,1280]{0,2,1:T(8,128)(2,1)S(1)}, u32[]{:S(2)}, u32[]{:S(2)}) async-start(bf16[256,4,1280]{0,2,1:T(8,128)(2,1)} %bitcast.132), calls=%async_computation.1 | async-start | bytes 5242880 | tf_op jit(solution)/shard_map/all_to_all | solution.py:145
  54.7 119.3 %all-gather.4.cloned.1.call-start = ((), (), s32[]{:S(2)}) async-start(), calls=%async_computation.4 | async-start | bytes 21626880 | tf_op jit(solution)/shard_map/all_gather | solution.py:34
  84.6 1.5 copy-start.5
  90.2 0.9 copy-start.3
  90.2 5.5 %copy-start.2 = (f32[4,10,128,128]{3,2,1,0:T(8,128)}, f32[4,10,128,128]{3,2,1,0:T(8,128)S(1)}, u32[]{:S(2)}) copy-start(f32[4,10,128,128]{3,2,1,0:T(8,128)S(1)} %get-tuple-element.492) | copy-start | bytes 7864324
  95.7 3.8 %copy-start.9 = (u32[128]{0:T(128)S(1)}, u32[128]{0:T(128)}, u32[]{:S(2)}) copy-start(u32[128]{0:T(128)} %constant.92) | copy-start | bytes 1540
  95.7 68.6 %all-to-all-start.2 = ((bf16[256,4,1280]{0,2,1:T(8,128)(2,1)}), bf16[256,4,1280]{0,2,1:T(8,128)(2,1)S(1)}, u32[]{:S(2)}, u32[]{:S(2)}) async-start(bf16[256,4,1280]{0,2,1:T(8,128)(2,1)} %bitcast.133), calls=%async_computation.2 | async-start | bytes 5242880 | tf_op jit(solution)/shard_map/all_to_all | solution.py:143
  164.4 2.3 copy-start.6
  241.7 4.0 %copy-start.4 = (f32[4,256,10,128]{1,3,2,0:T(8,128)S(1)}, f32[4,256,10,128]{1,3,2,0:T(8,128)}, u32[]{:S(2)}) copy-start(f32[4,256,10,128]{1,3,2,0:T(8,128)} %get-tuple-element.137) | copy-start | bytes 15728644
  287.4 4.4 %copy-start.1 = (f32[5120]{0:T(1024)S(1)}, f32[5120]{0:T(1024)}, u32[]{:S(2)}) copy-start(f32[5120]{0:T(1024)} %param.17) | copy-start | bytes 61444
Sparse Core Ops, SparseCore 0:
  91.2 82.7 all-gather.3
